TPU v7x, 512 devices: a whole 4x4x16 slice. The times are simulated.
512 devices in a mesh: ctx: 64 (over z, x), tp: 8 (over y, core).
Axes of the slice: x: 4, y: 4, z: 16, core: 2. Of those that a mesh axis runs over, the one named last changes fastest.
Arguments:
- tokens: bfloat16 [65536, 4096], P(('ctx', 'tp')), may hold values from -26 to 26
- query_weight: bfloat16 [4096, 2048], P('ctx', 'tp'), may hold values from -0.09375 to 0.09375
- kv_weight: bfloat16 [4096, 2048], P('ctx', 'tp'), may hold values from -0.09375 to 0.09375
- reach: int32 [1024], P('ctx'), may hold values from 1 to 2, as said below
- global_ids: int32 [2], replicated, may hold values from 0 to 1023, as said below
- rand_ids: int32 [1024, 3], replicated, may hold values from -1 to 1023, as said below
Outputs:
- attended: bfloat16 [65536, 2048], P('ctx', 'tp')
Inputs may be any that keep to these rules, and one draw needn't show every extreme that they name: Some query block has reach 2. `global_ids`: distinct block numbers; the last entry is block 1023. `rand_ids`: the -1 entries of a query block come after its other entries; the 16 query blocks of a run (blocks 16 * i to 16 * i + 15) list at most 2 entries, repeats counted, that name blocks of any one run; in some run all entries are filled and some run of key blocks is named by exactly 2 of them.
All inputs are finite; a program needn't handle non-finite values.
Results may differ from a plain program's by a relative error of at most 0.012.
The roundings to bfloat16 on the way count: a program that leaves them out, or rounds other values in their place, can miss the bound.
Values may be sent and summed in bfloat16 or wider, within the bound.
No kernel may reach another device: no remote copies, remote signals or barrier semaphores. Data moves between devices by JAX's collectives and lax.ppermute only.
A program may use at most 64 MiB of HBM per device.

v0:
```python
import jax
import jax.numpy as jnp
from jax import lax
from jax.sharding import PartitionSpec as P

HD = 128
GROUP = 2
BS = 64
WMAX = 2
G = 2
masked_score = -1e30


def with_halo(shard, sides, width):
    for axis, dim in sides:
        size, length = (lax.axis_size(axis), shard.shape[dim])
        up = [(i, (i + 1) % size) for i in range(size - 1)]
        down = [(j, i) for i, j in up]
        last = lax.slice_in_dim(shard, length - width, length, axis=dim)
        initial = lax.slice_in_dim(shard, 0, width, axis=dim)
        before = lax.ppermute(last, axis, up)
        after = lax.ppermute(initial, axis, down)
        shard = jnp.concatenate([before, shard, after], axis=dim)
    return shard


def attend_group(query_group, slab_group, valid_group, kv_local):
    group_blocks = query_group.shape[0]
    slot_count = slab_group.shape[1]
    queries = query_group.reshape(group_blocks, BS, kv_local, GROUP, HD)
    slabs = slab_group.reshape(group_blocks, slot_count, BS, kv_local, 2, HD)
    scores = jnp.einsum(
        "bqkgd,bsjkd->bkgqsj", queries, slabs[:, :, :, :, 0, :], preferred_element_type=jnp.float32
    )
    scores = scores.reshape(scores.shape[:4] + (slot_count * BS,)) * HD ** (-0.5)
    key_live = jnp.repeat(valid_group, BS, axis=1)
    scores = jnp.where(key_live[:, None, None, None, :], scores, masked_score)
    row_max = jnp.max(scores, axis=-1, keepdims=True)
    exponent = jnp.exp(scores - row_max)
    weights = (exponent / jnp.sum(exponent, axis=-1, keepdims=True)).astype(jnp.bfloat16)
    weights = weights.reshape(weights.shape[:4] + (slot_count, BS))
    mixed = jnp.einsum(
        "bkgqsj,bsjkd->bqkgd", weights, slabs[:, :, :, :, 1, :], preferred_element_type=jnp.float32
    )
    return mixed.astype(jnp.bfloat16).reshape(group_blocks * BS, kv_local * GROUP * HD)


def fetch_blocks(key_rows, global_ids, rand_ids, ctx_index, ctx_count):
    row_count, lane_width = key_rows.shape
    run_blocks = row_count // BS
    blocks = key_rows.reshape(run_blocks, BS, lane_width)
    padded = with_halo(key_rows, (("ctx", 0),), WMAX * BS)
    padded_blocks = padded.reshape(run_blocks + 2 * WMAX, BS, lane_width)
    window_kv = jnp.stack(
        [padded_blocks[shift_at : shift_at + run_blocks] for shift_at in range(2 * WMAX + 1)],
        axis=1,
    )
    global_owner = global_ids // run_blocks
    global_local = global_ids % run_blocks
    is_held = (global_owner == ctx_index)[:, None, None]
    sum_term = jnp.where(is_held, blocks[global_local].astype(jnp.float32), 0.0)
    global_kv = lax.psum(sum_term, "ctx").astype(jnp.bfloat16)
    slot_count = run_blocks * rand_ids.shape[1]
    capacity = max(2, (slot_count + ctx_count - 1) // ctx_count)
    listed = rand_ids.reshape(ctx_count, slot_count)
    owners = jnp.where(listed >= 0, listed // run_blocks, -1)
    owned_here = owners == ctx_index
    ranks = jnp.cumsum(owned_here.astype(jnp.int32), axis=1) - 1
    picks = owned_here[:, None, :] & (ranks[:, None, :] == jnp.arange(capacity)[None, :, None])
    local_ids = jnp.sum(jnp.where(picks, listed[:, None, :] % run_blocks, 0), axis=2)
    filled = jnp.any(picks, axis=2)
    outgoing = jnp.where(filled[:, :, None, None], blocks[local_ids], jnp.zeros((), jnp.bfloat16))
    incoming = lax.all_to_all(outgoing, "ctx", split_axis=0, concat_axis=0, tiled=True)
    wanted = lax.dynamic_index_in_dim(owners, ctx_index, 0, keepdims=False)
    slot_order = jnp.arange(slot_count)
    earlier = (wanted[None, :] == wanted[:, None]) & (slot_order[None, :] < slot_order[:, None])
    position = jnp.sum(earlier.astype(jnp.int32), axis=1)
    flat_index = jnp.where(wanted >= 0, wanted * capacity + position, 0)
    random_kv = incoming.reshape(ctx_count * capacity, BS, lane_width)[flat_index]
    random_kv = random_kv.reshape(run_blocks, -1, BS, lane_width)
    return (window_kv, global_kv, random_kv)


def per_device(tokens, query_weight, kv_weight, reach, global_ids, rand_ids):
    ctx_count = lax.axis_size("ctx")
    ctx_index = lax.axis_index("ctx")
    full_query_w, full_kv_w = (
        lax.all_gather(query_weight, "ctx", axis=0, tiled=True),
        lax.all_gather(kv_weight, "ctx", axis=0, tiled=True),
    )
    query_width = full_query_w.shape[1]
    token_piece = lax.all_gather(tokens, "tp", axis=0, tiled=True)
    query_part = jnp.dot(token_piece, full_query_w, preferred_element_type=jnp.float32)
    key_part = jnp.dot(token_piece, full_kv_w, preferred_element_type=jnp.float32)
    projected = jnp.concatenate([query_part, key_part], axis=1)
    query_rows = projected[:, :query_width].astype(jnp.bfloat16)
    key_rows = projected[:, query_width:].astype(jnp.bfloat16)
    window_kv, global_kv, random_kv = fetch_blocks(
        key_rows, global_ids, rand_ids, ctx_index, ctx_count
    )
    row_count, lane_width = key_rows.shape
    run_blocks = row_count // BS
    kv_local = lane_width // (2 * HD)
    offsets = jnp.arange(-WMAX, WMAX + 1)
    first_block = ctx_index * run_blocks
    target = first_block + jnp.arange(run_blocks)[:, None] + offsets[None, :]
    window_live = (
        (jnp.abs(offsets)[None, :] <= reach[:, None])
        & (target >= 0)
        & (target < run_blocks * ctx_count)
    )
    own_lists = lax.dynamic_slice_in_dim(rand_ids, first_block, run_blocks, 0)
    slot_valid = jnp.concatenate(
        [window_live, jnp.ones((run_blocks, G), jnp.bool_), own_lists >= 0], axis=1
    )
    global_tiled = jnp.broadcast_to(global_kv[None], (run_blocks,) + global_kv.shape)
    slab_all = jnp.concatenate([window_kv, global_tiled, random_kv], axis=1)
    slot_total = slab_all.shape[1]
    group_size = max((divisor for divisor in range(1, 9) if run_blocks % divisor == 0))
    group_count = run_blocks // group_size
    query_groups = query_rows.reshape(group_count, group_size, BS, query_width)
    slab_groups = slab_all.reshape(group_count, group_size, slot_total, BS, lane_width)
    valid_groups = slot_valid.reshape(group_count, group_size, slot_total)

    def one_group(operands):
        return attend_group(operands[0], operands[1], operands[2], kv_local)

    outputs = lax.map(one_group, (query_groups, slab_groups, valid_groups))
    return outputs.reshape(row_count, query_width)


def solution(mesh):
    in_specs = (P(("ctx", "tp"), None), P("ctx", "tp"), P("ctx", "tp"), P("ctx"), P(), P())
    out_specs = P("ctx", "tp")
    return jax.shard_map(
        per_device, mesh=mesh, in_specs=in_specs, out_specs=out_specs, check_vma=False
    )
```

profile of v0, /device:TPU:8, one launch (start us, length us, event | category | flops | bytes accessed | tf_op | source)
XLA Modules:
  0.0 769.2 jit_solution(11982867577212984012)
XLA Ops:
  6.5 0.7 all-gather.6.cloned.1.call-update
  7.3 0.0 all-gather.4.cloned.1.call-start
  7.3 0.7 all-gather.4.cloned.1.call-update
  8.0 0.9 copy.68
  9.0 0.3 reshape.282
  9.2 0.1 copy.72
  9.3 0.2 reduce_window_sum.11
  9.6 0.1 copy.70
  9.6 0.1 copy.69
  9.8 0.1 copy.71
  9.9 0.1 copy.73
  10.0 0.1 reshape.297
  10.2 0.7 compare_select_fusion.2
  10.9 144.8 %all-gather.6.cloned.1.call-done = bf16[4096,256]{1,0:T(8,128)(2,1)} async-done(((bf16[64,256]{1,0:T(8,128)(2,1)}), bf16[4096,256]{1,0:T(8,128)(2,1)}) %all-gather.6.cloned.1.call-update) | async-done | bytes 2097168 | tf_op jit(solution)/shard_map/all_gather | solution.py:89
  155.7 54.8 %all-gather.4.cloned.1.call-done = bf16[1024,4096]{1,0:T(8,128)(2,1)} async-done(((bf16[128,4096]{1,0:T(8,128)(2,1)}), bf16[1024,4096]{1,0:T(8,128)(2,1)}) %all-gather.4.cloned.1.call-update) | async-done | bytes 8388624 | tf_op jit(solution)/shard_map/all_gather | solution.py:92
  210.4 6.3 convolution_convert_fusion.1
  216.8 2.7 gather_fusion.1
  219.5 4.5 broadcast_select_fusion
  224.0 16.0 %all-to-all-start = ((bf16[64,2,64,256]{3,2,1,0:T(8,128)(2,1)}), bf16[64,2,64,256]{3,2,1,0:T(8,128)(2,1)}, u32[]{:S(2)}, u32[]{:S(2)}) async-start(bf16[64,2,64,256]{3,2,1,0:T(8,128)(2,1)} %broadcast_select_fusion), calls=%async_computation | async-start | bytes 8388608 | tf_op jit(solution)/shard_map/all_to_all | solution.py:73
  240.0 0.0 all-gather.8.cloned.1.call-start
  240.1 0.7 all-gather.8.cloned.1.call-update
  240.8 0.1 pad.1.clone
  240.9 0.8 dynamic-slice_compare_fusion
  241.6 0.1 fusion.35
  241.7 0.1 pad_add_fusion
  241.8 0.1 copy.79
  241.9 0.2 convert_reduce_fusion
  242.1 1.3 collective-permute-start.1
  243.4 4.5 collective-permute-start
  248.0 0.6 gather_fusion
  248.6 0.1 convert_select_fusion
  248.6 184.2 %all-gather.8.cloned.1.call-done = bf16[4096,256]{1,0:T(8,128)(2,1)} async-done(((bf16[64,256]{1,0:T(8,128)(2,1)}), bf16[4096,256]{1,0:T(8,128)(2,1)}) %all-gather.8.cloned.1.call-update) | async-done | bytes 2097168 | tf_op jit(solution)/shard_map/all_gather | solution.py:88
  432.9 6.3 convolution_convert_fusion
  439.2 279.7 %all-reduce.1 = bf16[2,64,256]{2,1,0:T(8,128)(2,1)S(1)} all-reduce(f32[2,64,256]{2,1,0:T(8,128)S(1)} %convert_select_fusion), channel_id=1, replica_groups=mesh['ctx'=64,'tp'=8] {'ctx'}, use_global_device_ids=true, to_apply=%region_0.1 | all-reduce | flops 32768 | bytes 196608 | tf_op jit(solution)/shard_map/psum | solution.py:62
  718.9 0.1 pad_maximum_fusion
  719.1 0.9 constant_dynamic-update-slice_fusion.6
  720.0 0.9 constant_dynamic-update-slice_fusion.5
  720.8 0.9 constant_dynamic-update-slice_fusion.4
  721.7 0.9 constant_dynamic-update-slice_fusion.3
  722.6 0.9 constant_dynamic-update-slice_fusion.2
  723.4 1.1 broadcast_dynamic-update-slice_fusion
  724.5 2.8 gather_fusion.2
  727.4 1.3 constant_dynamic-update-slice_fusion.1
  728.7 34.0 %while.10 = (s32[]{:T(128)}, bf16[2,512,256]{2,1,0:T(8,128)(2,1)}, bf16[2,8,10,64,256]{4,3,2,1,0:T(8,128)(2,1)}, pred[2,8,10]{2,1,0:T(8,128)(4,1)S(1)}, bf16[2,8,64,256]{3,2,1,0:T(8,128)(2,1)S(1)}, /*index=5*/s32[]{:T(128)}) while((s32[]{:T(128)}, bf16[2,512,256]{2,1,0:T(8,128)(2,1)}, bf16[2,8,10,64,256]{4,3,2,1,0:T(8,128)(2,1)}, ...), condition=%wide.region_8.9_spmd, body=%wide.region_5.8_spmd.sunk | while | flops 343537664 | bytes 33575460 | solution.py:128
  728.7 0.1 reshape.319
  728.8 3.6 constant_dynamic-slice_fusion.6
  732.3 3.5 reshape.320
  735.9 3.7 fusion.55
  739.6 1.3 bitcast_reduce_fusion.2
  740.9 1.5 fusion.56
  742.4 1.9 fusion.57
  744.4 0.3 copy.115
  744.6 0.2 broadcast_in_dim.143
  744.9 0.8 copy-done.2
  745.7 0.1 reshape.319
  745.7 3.6 constant_dynamic-slice_fusion.6
  749.3 3.5 reshape.320
  752.9 3.7 fusion.55
  756.6 1.3 bitcast_reduce_fusion.2
  757.9 1.5 fusion.56
  759.4 1.9 fusion.57
  761.3 0.3 copy.115
  761.6 0.2 broadcast_in_dim.143
  761.9 0.8 copy-done.2
  (36 shorter events, 0.3 us)
Async XLA Ops:
  6.5 149.1 %all-gather.6.cloned.1.call-start = ((), (), s32[]{:S(2)}) async-start(), calls=%async_computation.2 | async-start | bytes 2129920 | tf_op jit(solution)/shard_map/all_gather | solution.py:89
  7.3 203.2 %all-gather.4.cloned.1.call-start = ((), (), s32[]{:S(2)}) async-start(), calls=%async_computation.1 | async-start | bytes 9437184 | tf_op jit(solution)/shard_map/all_gather | solution.py:92
  224.0 17.6 %copy-start = (s32[16]{0:T(128)S(1)}, s32[16]{0:T(128)}, u32[]{:S(2)}) copy-start(s32[16]{0:T(128)} %param.11) | copy-start | bytes 196
  224.0 18.1 %copy-start.3 = (s32[2]{0:T(128)S(1)}, s32[2]{0:T(128)}, u32[]{:S(2)}) copy-start(s32[2]{0:T(128)} %param.12) | copy-start | bytes 28
  224.0 500.5 %all-to-all-start = ((bf16[64,2,64,256]{3,2,1,0:T(8,128)(2,1)}), bf16[64,2,64,256]{3,2,1,0:T(8,128)(2,1)}, u32[]{:S(2)}, u32[]{:S(2)}) async-start(bf16[64,2,64,256]{3,2,1,0:T(8,128)(2,1)} %broadcast_select_fusion), calls=%async_computation | async-start | bytes 8388608 | tf_op jit(solution)/shard_map/all_to_all | solution.py:73
  240.0 192.9 %all-gather.8.cloned.1.call-start = ((), (), s32[]{:S(2)}) async-start(), calls=%async_computation.3 | async-start | bytes 2129920 | tf_op jit(solution)/shard_map/all_gather | solution.py:88
  242.1 476.8 %collective-permute-start.1 = (bf16[128,256]{1,0:T(8,128)(2,1)S(1)}, bf16[128,256]{1,0:T(8,128)(2,1)S(1)}, u32[]{:S(2)}, u32[]{:S(2)}) collective-permute-start(bf16[128,256]{1,0:T(8,128)(2,1)S(1)} %get-tuple-element.61), channel_id=1, source_target_pairs={{8,0},{16,8},{24,16},{32,24},{40,32},{48,40},{56,48},{64,56},{72,6... | collective-permute-start | bytes 196616 | tf_op jit(solution)/shard_map/ppermute | solution.py:22
  243.4 475.5 %collective-permute-start = (bf16[128,256]{1,0:T(8,128)(2,1)S(1)}, bf16[128,256]{1,0:T(8,128)(2,1)S(1)}, u32[]{:S(2)}, u32[]{:S(2)}) collective-permute-start(bf16[128,256]{1,0:T(8,128)(2,1)S(1)} %get-tuple-element.62), channel_id=1, source_target_pairs={{0,8},{8,16},{16,24},{24,32},{32,40},{40,48},{48,56},{56,64},{64,7... | collective-permute-start | bytes 196616 | tf_op jit(solution)/shard_map/ppermute | solution.py:21
  742.4 2.4 copy-start.1
  744.9 0.8 copy-start.2
  759.4 2.4 copy-start.1
  761.8 0.8 copy-start.2
Sparse Core Ops, SparseCore 0:
  10.3 145.3 all-gather.5
  157.8 52.5 all-gather.3
  243.8 189.0 all-gather.7
where the time goes:
time: 770 us; the launch traced here: 769 us
  waiting for transfers between devices  386 us (50%)
  blocking collectives  280 us (36%)
  local copies, waits for them, and re-layouts  39.2 us (5%)
  starting transfers between devices  21.9 us (3%)
  matrix products  19 us (2%)
  between operations  13.3 us (2%)
  other arithmetic  9.89 us (1%)
    psum x1, blocking collectives, fetch_blocks(): global_kv = lax.psum(sum_term, 'ctx').astype(jnp.bfloat16)  280 us
    all_gather x1, waiting for transfers between devices, per_device(): lax.all_gather(query_weight, 'ctx', axis=0, tiled=True)  184 us
    all_gather x1, waiting for transfers between devices, per_device(): lax.all_gather(kv_weight, 'ctx', axis=0, tiled=True)  145 us
    all_gather x1, waiting for transfers between devices, per_device(): token_piece = lax.all_gather(tokens, 'tp', axis=0, tiled=True)  54.8 us
    all_to_all x1, starting transfers between devices, fetch_blocks(): lax.all_to_all(outgoing, 'ctx', split_axis=0, concat_axis=0, tiled=True)  16 us
  transfers between devices with their start and end apart: 6, of which 3 were waited for; matrix products, arithmetic and copies ran while one was open for 2% of the time, Pallas kernels for 0%

commit v1 on v0

--- a/solution.py
+++ b/solution.py
@@ -1,3 +1,4 @@
+import functools
 import jax
 import jax.numpy as jnp
 from jax import lax
@@ -9,6 +10,17 @@
 WMAX = 2
 G = 2
 masked_score = -1e30
+
+
+def do_things(arr, array_axis):
+    r_now = lax.all_to_all(
+        jnp.stack(lax.axis_size("ctx") * [arr]), axis_name="ctx", concat_axis=0, split_axis=0
+    )
+    x_next = jnp.concatenate(r_now, array_axis)
+    return x_next
+
+
+columns_form = functools.partial(do_things, array_axis=0)
 
 
 def with_halo(shard, sides, width):
@@ -86,7 +98,7 @@
     ctx_index = lax.axis_index("ctx")
     full_query_w, full_kv_w = (
         lax.all_gather(query_weight, "ctx", axis=0, tiled=True),
-        lax.all_gather(kv_weight, "ctx", axis=0, tiled=True),
+        columns_form(kv_weight),
     )
     query_width = full_query_w.shape[1]
     token_piece = lax.all_gather(tokens, "tp", axis=0, tiled=True)

time: 770 us -> 683 us (0.89)
  the two profiles are of different devices: /device:TPU:8 before, /device:TPU:24 now
where the time goes in v1:
time: 683 us; the launch traced here: 682 us
  waiting for transfers between devices  287 us (42%)
  blocking collectives  282 us (41%)
  local copies, waits for them, and re-layouts  40.9 us (6%)
  starting transfers between devices  30.7 us (4%)
  matrix products  18.4 us (3%)
  between operations  15 us (2%)
  other arithmetic  8.55 us (1%)
    psum x1, blocking collectives, fetch_blocks(): global_kv = lax.psum(sum_term, 'ctx').astype(jnp.bfloat16)  282 us
    all_gather x1, waiting for transfers between devices, per_device(): lax.all_gather(query_weight, 'ctx', axis=0, tiled=True)  187 us
    all_to_all x1, waiting for transfers between devices, do_things(): lax.all_to_all(jnp.stack(lax.axis_size('ctx') * [arr]), axis_name='ctx',...  98.7 us
    all_to_all x1, starting transfers between devices, do_things(): lax.all_to_all(jnp.stack(lax.axis_size('ctx') * [arr]), axis_name='ctx',...  18.6 us
  transfers between devices with their start and end apart: 6, of which 2 were waited for; matrix products, arithmetic and copies ran while one was open for 2% of the time, Pallas kernels for 0%

profile of v1, /device:TPU:24, one launch (start us, length us, event | category | flops | bytes accessed | tf_op | source)
XLA Modules:
  0.0 682.4 jit_solution(6954795083290051320)
XLA Ops:
  7.4 0.7 all-gather.3.cloned.1.call-update
  8.1 2.4 stack.2
  10.5 18.6 %all-to-all-start = ((bf16[64,64,256]{2,1,0:T(8,128)(2,1)}), bf16[64,64,256]{2,1,0:T(8,128)(2,1)S(1)}, u32[]{:S(2)}, u32[]{:S(2)}) async-start(bf16[64,64,256]{2,1,0:T(8,128)(2,1)} %stack.2), calls=%async_computation | async-start | bytes 4194304 | tf_op jit(solution)/shard_map/all_to_all | solution.py:16
  29.0 0.2 copy.68
  29.3 0.3 reshape.288
  29.5 0.1 copy.72
  29.7 0.2 reduce_window_sum.11
  29.9 0.1 copy.70
  30.0 0.1 copy.69
  30.1 0.1 copy.71
  30.3 0.1 copy.73
  30.3 0.1 reshape.303
  30.5 98.7 %all-to-all-done = bf16[64,64,256]{2,1,0:T(8,128)(2,1)S(1)} async-done(((bf16[64,64,256]{2,1,0:T(8,128)(2,1)}), bf16[64,64,256]{2,1,0:T(8,128)(2,1)S(1)}, u32[]{:S(2)}, u32[]{:S(2)}) %all-to-all-start) | async-done | bytes 2097184 | tf_op jit(solution)/shard_map/all_to_all | solution.py:16
  129.3 5.7 convolution_convert_fusion.1
  135.0 2.7 gather_fusion.1
  137.7 4.5 broadcast_select_fusion
  142.2 6.2 all-to-all-start.1
  148.4 0.0 all-gather.5.cloned.1.call-start
  148.5 0.5 all-gather.5.cloned.1.call-update
  149.0 0.1 pad.1.clone
  149.1 0.1 dynamic-slice_compare_fusion
  149.2 0.1 fusion.35
  149.3 0.1 pad_add_fusion
  149.4 0.1 copy.79
  149.5 0.2 convert_reduce_fusion
  149.7 0.6 gather_fusion
  150.3 0.1 convert_select_fusion
  150.4 1.3 collective-permute-start.1
  151.7 4.5 collective-permute-start
  156.2 187.1 %all-gather.5.cloned.1.call-done = bf16[4096,256]{1,0:T(8,128)(2,1)} async-done(((bf16[64,256]{1,0:T(8,128)(2,1)}), bf16[4096,256]{1,0:T(8,128)(2,1)}) %all-gather.5.cloned.1.call-update) | async-done | bytes 2097168 | tf_op jit(solution)/shard_map/all_gather | solution.py:100
  343.3 6.3 convolution_convert_fusion
  349.6 281.7 %all-reduce.1 = bf16[2,64,256]{2,1,0:T(8,128)(2,1)S(1)} all-reduce(f32[2,64,256]{2,1,0:T(8,128)S(1)} %convert_select_fusion), channel_id=1, replica_groups=mesh['ctx'=64,'tp'=8] {'ctx'}, use_global_device_ids=true, to_apply=%region_0.1 | all-reduce | flops 32768 | bytes 196608 | tf_op jit(solution)/shard_map/psum | solution.py:74
  631.3 0.1 pad_maximum_fusion
  631.4 0.9 constant_dynamic-update-slice_fusion.6
  632.3 0.9 constant_dynamic-update-slice_fusion.5
  633.2 0.9 constant_dynamic-update-slice_fusion.4
  634.0 0.9 constant_dynamic-update-slice_fusion.3
  634.9 0.9 constant_dynamic-update-slice_fusion.2
  635.8 1.1 broadcast_dynamic-update-slice_fusion
  636.9 2.8 gather_fusion.2
  639.7 1.3 constant_dynamic-update-slice_fusion.1
  641.0 34.0 %while.10 = (s32[]{:T(128)}, bf16[2,512,256]{2,1,0:T(8,128)(2,1)}, bf16[2,8,10,64,256]{4,3,2,1,0:T(8,128)(2,1)}, pred[2,8,10]{2,1,0:T(8,128)(4,1)S(1)}, bf16[2,8,64,256]{3,2,1,0:T(8,128)(2,1)S(1)}, /*index=5*/s32[]{:T(128)}) while((s32[]{:T(128)}, bf16[2,512,256]{2,1,0:T(8,128)(2,1)}, bf16[2,8,10,64,256]{4,3,2,1,0:T(8,128)(2,1)}, ...), condition=%wide.region_8.9_spmd, body=%wide.region_5.8_spmd.sunk | while | flops 343537664 | bytes 33575460 | solution.py:140
  641.0 0.1 reshape.325
  641.1 3.6 constant_dynamic-slice_fusion.6
  644.7 3.5 reshape.326
  648.2 3.7 fusion.55
  651.9 1.3 bitcast_reduce_fusion.2
  653.2 1.5 fusion.56
  654.8 0.0 copy-start.2
  654.8 1.9 fusion.57
  656.7 0.3 copy.115
  657.0 0.2 broadcast_in_dim.143
  657.2 0.0 copy-start.3
  657.2 0.8 copy-done.3
  658.0 0.1 reshape.325
  658.1 3.6 constant_dynamic-slice_fusion.6
  661.7 3.5 reshape.326
  665.2 3.7 fusion.55
  668.9 1.3 bitcast_reduce_fusion.2
  670.2 1.5 fusion.56
  671.8 1.9 fusion.57
  673.7 0.3 copy.115
  674.0 0.2 broadcast_in_dim.143
  674.2 0.8 copy-done.3
  (38 shorter events, 0.3 us)
Async XLA Ops:
  7.4 21.7 %copy-start = (s32[1024,3]{0,1:T(4,128)S(1)}, s32[1024,3]{0,1:T(4,128)}, u32[]{:S(2)}) copy-start(s32[1024,3]{0,1:T(4,128)} %param.13) | copy-start | bytes 36868
  7.4 23.1 %copy-start.4 = (s32[2]{0:T(128)S(1)}, s32[2]{0:T(128)}, u32[]{:S(2)}) copy-start(s32[2]{0:T(128)} %param.12) | copy-start | bytes 28
  7.4 121.9 %all-gather.3.cloned.1.call-start = ((), (), s32[]{:S(2)}) async-start(), calls=%async_computation.2 | async-start | bytes 9437184 | tf_op jit(solution)/shard_map/all_gather | solution.py:104
  10.5 118.8 %all-to-all-start = ((bf16[64,64,256]{2,1,0:T(8,128)(2,1)}), bf16[64,64,256]{2,1,0:T(8,128)(2,1)S(1)}, u32[]{:S(2)}, u32[]{:S(2)}) async-start(bf16[64,64,256]{2,1,0:T(8,128)(2,1)} %stack.2), calls=%async_computation | async-start | bytes 4194304 | tf_op jit(solution)/shard_map/all_to_all | solution.py:16
  142.2 7.0 %copy-start.1 = (s32[16]{0:T(128)S(1)}, s32[16]{0:T(128)}, u32[]{:S(2)}) copy-start(s32[16]{0:T(128)} %param.11) | copy-start | bytes 196
  142.2 494.7 %all-to-all-start.1 = ((bf16[64,2,64,256]{3,2,1,0:T(8,128)(2,1)}), bf16[64,2,64,256]{3,2,1,0:T(8,128)(2,1)}, u32[]{:S(2)}, u32[]{:S(2)}) async-start(bf16[64,2,64,256]{3,2,1,0:T(8,128)(2,1)} %broadcast_select_fusion), calls=%async_computation.1 | async-start | bytes 8388608 | tf_op jit(solution)/shard_map/all_to_all | solution.py:85
  148.4 194.8 %all-gather.5.cloned.1.call-start = ((), (), s32[]{:S(2)}) async-start(), calls=%async_computation.3 | async-start | bytes 2129920 | tf_op jit(solution)/shard_map/all_gather | solution.py:100
  150.4 480.9 %collective-permute-start.1 = (bf16[128,256]{1,0:T(8,128)(2,1)S(1)}, bf16[128,256]{1,0:T(8,128)(2,1)S(1)}, u32[]{:S(2)}, u32[]{:S(2)}) collective-permute-start(bf16[128,256]{1,0:T(8,128)(2,1)S(1)} %get-tuple-element.61), channel_id=1, source_target_pairs={{8,0},{16,8},{24,16},{32,24},{40,32},{48,40},{56,48},{64,56},{72,6... | collective-permute-start | bytes 196616 | tf_op jit(solution)/shard_map/ppermute | solution.py:34
  151.7 479.6 %collective-permute-start = (bf16[128,256]{1,0:T(8,128)(2,1)S(1)}, bf16[128,256]{1,0:T(8,128)(2,1)S(1)}, u32[]{:S(2)}, u32[]{:S(2)}) collective-permute-start(bf16[128,256]{1,0:T(8,128)(2,1)S(1)} %get-tuple-element.62), channel_id=1, source_target_pairs={{0,8},{8,16},{16,24},{24,32},{32,40},{40,48},{48,56},{56,64},{64,7... | collective-permute-start | bytes 196616 | tf_op jit(solution)/shard_map/ppermute | solution.py:33
  654.8 2.4 copy-start.2
  657.2 0.8 copy-start.3
  671.8 2.4 copy-start.2
  674.2 0.8 copy-start.3
Sparse Core Ops, SparseCore 0:
  10.3 59.7 all-gather.2
Sparse Core Ops, SparseCore 1:
  151.9 191.4 all-gather.4
